TPU v7x, 256 devices: a whole 4x4x8 slice. The times are simulated.
256 devices in a mesh: dp: 8 (over x, core), seq: 32 (over y, z).
Axes of the slice: x: 4, y: 4, z: 8, core: 2. Of those that a mesh axis runs over, the one named last changes fastest.
Arguments:
- probe_vectors: float32 [8, 4096, 2048], P('dp', 'seq'), may hold values from -8 to 8
- lookup_vectors: float32 [8, 4096, 2048], P('dp', 'seq'), may hold values from -8 to 8
- payload_vectors: float32 [8, 4096, 2048], P('dp', 'seq'), may hold values from -8 to 8
- channel_sharpness: float32 [16], replicated, may hold values from 0.7 to 1.4
- adjacent_tiles: int32 [8, 32, 4], P('dp'), may hold values from 0 to 31, as said below
- output_adjoint: float32 [8, 4096, 2048], P('dp', 'seq'), may hold values from -16 to 16
Outputs:
- context_output: float32 [8, 4096, 2048], P('dp', 'seq')
- probe_derivative: float32 [8, 4096, 2048], P('dp', 'seq')
- lookup_derivative: float32 [8, 4096, 2048], P('dp', 'seq')
- payload_derivative: float32 [8, 4096, 2048], P('dp', 'seq')
- channel_sharpness_derivative: float32 [16], replicated
Inputs may be any that keep to these rules, and one draw needn't show every extreme that they name: `adjacent_tiles`: row b of each sequence lists b first, then b - 1 and b + 1 modulo 32, then one further block; the 4 entries of a row are distinct.
All inputs are finite; a program needn't handle non-finite values.
Results may differ from a plain program's by a relative error of at most 0.0003.
Values sent between devices are 32-bit elements; how exact they have to be, the bound alone decides.
A program may use at most 128 MiB of HBM per device.

v0:
```python
import math

import jax
import jax.numpy as jnp
from jax import lax
from jax.sharding import PartitionSpec as P

RESIDENT_CHANNELS = 16
HD = 128
BLOCK = 128


def fetch_listed(key_blocks, value_blocks, wanted):
    key_table, value_table = (
        lax.all_to_all(key_blocks, "seq", split_axis=1, concat_axis=0, tiled=True),
        lax.all_to_all(value_blocks, "seq", split_axis=1, concat_axis=0, tiled=True),
    )
    key_send = jnp.take(key_table, wanted, axis=0)
    value_send = jnp.take(value_table, wanted, axis=0)
    key_got, value_got = (
        lax.all_to_all(key_send, "seq", split_axis=0, concat_axis=2, tiled=True),
        lax.all_to_all(value_send, "seq", split_axis=0, concat_axis=2, tiled=True),
    )
    return (key_got[0], value_got[0])


def return_listed(key_terms, value_terms, wanted, total_blocks):
    key_pieces, value_pieces = (
        lax.all_to_all(key_terms, "seq", split_axis=1, concat_axis=0, tiled=True),
        lax.all_to_all(value_terms, "seq", split_axis=1, concat_axis=0, tiled=True),
    )
    block_ids = wanted.reshape(-1)
    one_hot = (jnp.arange(total_blocks, dtype=jnp.int32)[:, None] == block_ids[None, :]).astype(
        jnp.float32
    )
    piece_rows = key_pieces.shape[1]
    features = key_pieces.shape[2]
    key_summed = jnp.dot(
        one_hot, key_pieces.reshape(block_ids.shape[0], -1), precision=lax.Precision.HIGHEST
    )
    value_summed = jnp.dot(
        one_hot, value_pieces.reshape(block_ids.shape[0], -1), precision=lax.Precision.HIGHEST
    )
    key_summed = key_summed.reshape(total_blocks, piece_rows, features)
    value_summed = value_summed.reshape(total_blocks, piece_rows, features)
    key_back, value_back = (
        lax.all_to_all(key_summed, "seq", split_axis=0, concat_axis=1, tiled=True),
        lax.all_to_all(value_summed, "seq", split_axis=0, concat_axis=1, tiled=True),
    )
    return (key_back, value_back)


def per_device(
    probe_vectors,
    lookup_vectors,
    payload_vectors,
    channel_sharpness,
    adjacent_tiles,
    output_adjoint,
):
    devices = lax.axis_size("seq")
    features = probe_vectors.shape[2]
    own_blocks = probe_vectors.shape[1] // BLOCK
    total_blocks = own_blocks * devices
    adjacent_tile_lines = adjacent_tiles[0]
    key_blocks = lookup_vectors[0].reshape(own_blocks, BLOCK, features)
    value_blocks = payload_vectors[0].reshape(own_blocks, BLOCK, features)
    first_slot = 1
    near_key = key_blocks[:, None]
    near_value = value_blocks[:, None]
    wanted = adjacent_tile_lines[:, first_slot:]
    far_key, far_value = fetch_listed(key_blocks, value_blocks, wanted)
    far_key = far_key.reshape(own_blocks, -1, BLOCK, features)
    far_value = far_value.reshape(own_blocks, -1, BLOCK, features)
    listed_key = jnp.concatenate([near_key, far_key], axis=1).reshape(
        own_blocks, -1, RESIDENT_CHANNELS, HD
    )
    listed_value = jnp.concatenate([near_value, far_value], axis=1).reshape(
        own_blocks, -1, RESIDENT_CHANNELS, HD
    )
    reciprocal_dimension_sqrt = 1.0 / math.sqrt(HD)
    head_factor = channel_sharpness * reciprocal_dimension_sqrt
    query_heads = probe_vectors[0].reshape(own_blocks, BLOCK, RESIDENT_CHANNELS, HD)
    scaled_queries = query_heads * head_factor[None, None, :, None]
    sharpened_logits = jnp.einsum(
        "lqhd,lkhd->lhqk", scaled_queries, listed_key, precision=lax.Precision.HIGHEST
    )
    row_max = jnp.max(sharpened_logits, axis=-1, keepdims=True)
    shifted = jnp.exp(sharpened_logits - row_max)
    inverse_total = 1.0 / jnp.sum(shifted, axis=-1, keepdims=True)
    normalized_probabilities = shifted * inverse_total
    context_output = jnp.einsum(
        "lhqk,lkhd->lqhd", normalized_probabilities, listed_value, precision=lax.Precision.HIGHEST
    )
    grad_heads = output_adjoint[0].reshape(own_blocks, BLOCK, RESIDENT_CHANNELS, HD)
    row_dot = jnp.sum(grad_heads * context_output, axis=-1)
    prob_grad = jnp.einsum(
        "lqhd,lkhd->lhqk", grad_heads, listed_value, precision=lax.Precision.HIGHEST
    )
    logit_derivative = normalized_probabilities * (
        prob_grad - jnp.transpose(row_dot, (0, 2, 1))[..., None]
    )
    sharpness_contributions = (
        jnp.sum(logit_derivative * sharpened_logits, axis=(0, 2, 3)) / channel_sharpness
    )
    probe_derivative = (
        jnp.einsum("lhqk,lkhd->lqhd", logit_derivative, listed_key, precision=lax.Precision.HIGHEST)
        * head_factor[None, None, :, None]
    )
    listed_key_grad = jnp.einsum(
        "lhqk,lqhd->lkhd", logit_derivative, scaled_queries, precision=lax.Precision.HIGHEST
    )
    listed_value_grad = jnp.einsum(
        "lhqk,lqhd->lkhd", normalized_probabilities, grad_heads, precision=lax.Precision.HIGHEST
    )
    listed_key_grad = listed_key_grad.reshape(own_blocks, -1, BLOCK, features)
    listed_value_grad = listed_value_grad.reshape(own_blocks, -1, BLOCK, features)
    own_key_grad = listed_key_grad[:, 0]
    own_value_grad = listed_value_grad[:, 0]
    far_key_terms = listed_key_grad[:, first_slot:].reshape(-1, BLOCK, features)
    far_value_terms = listed_value_grad[:, first_slot:].reshape(-1, BLOCK, features)
    key_back, value_back = return_listed(far_key_terms, far_value_terms, wanted, total_blocks)
    own_key_grad = own_key_grad + key_back
    own_value_grad = own_value_grad + value_back
    channel_sharpness_derivative = lax.psum(sharpness_contributions, ("dp", "seq"))
    rows = own_blocks * BLOCK
    return (
        context_output.reshape(1, rows, features),
        probe_derivative.reshape(1, rows, features),
        own_key_grad,
        own_value_grad,
        channel_sharpness_derivative,
    )


def solution(mesh):
    placed = (
        P("dp", "seq", None),
        P("dp", "seq", None),
        P("dp", "seq", None),
        P(),
        P("dp", None, None),
        P("dp", "seq", None),
    )
    return jax.shard_map(
        per_device,
        mesh=mesh,
        in_specs=placed,
        out_specs=(
            P("dp", "seq", None),
            P("dp", "seq", None),
            P("dp", "seq", None),
            P("dp", "seq", None),
            P(),
        ),
        check_vma=False,
    )
```

profile of v0, /device:TPU:1, one launch (start us, length us, event | category | flops | bytes accessed | tf_op | source)
XLA Modules:
  0.0 595.0 jit_solution(5770133682942922079)
XLA Ops:
  0.7 3.4 copy.129
  4.0 12.0 %all-to-all-start.2 = ((f32[1,128,2048]{2,0,1:T(1,128)}), f32[1,128,2048]{2,0,1:T(1,128)S(1)}, u32[]{:S(2)}, u32[]{:S(2)}) async-start(f32[1,128,2048]{2,0,1:T(1,128)} %copy.129), calls=%async_computation.2 | async-start | bytes 2097152 | tf_op jit(solution)/shard_map/all_to_all | solution.py:15
  18.1 22.6 %all-to-all-done.2 = f32[1,128,2048]{2,0,1:T(1,128)S(1)} async-done(((f32[1,128,2048]{2,0,1:T(1,128)}), f32[1,128,2048]{2,0,1:T(1,128)S(1)}, u32[]{:S(2)}, u32[]{:S(2)}) %all-to-all-start.2) | async-done | bytes 1048608 | tf_op jit(solution)/shard_map/all_to_all | solution.py:15
  40.7 8.8 %all-to-all-start = ((f32[1,128,2048]{2,0,1:T(1,128)}), f32[1,128,2048]{2,0,1:T(1,128)S(1)}, u32[]{:S(2)}, u32[]{:S(2)}) async-start(f32[1,128,2048]{2,0,1:T(1,128)} %copy.123), calls=%async_computation | async-start | bytes 2097152 | tf_op jit(solution)/shard_map/all_to_all | solution.py:16
  49.8 2.5 reduce.8
  52.6 21.6 %all-to-all-done = f32[1,128,2048]{2,0,1:T(1,128)S(1)} async-done(((f32[1,128,2048]{2,0,1:T(1,128)}), f32[1,128,2048]{2,0,1:T(1,128)S(1)}, u32[]{:S(2)}, u32[]{:S(2)}) %all-to-all-start) | async-done | bytes 1048608 | tf_op jit(solution)/shard_map/all_to_all | solution.py:16
  74.2 2.5 reduce.7
  77.0 4.0 gather_fusion.1
  81.1 4.1 gather_fusion
  85.1 6.8 %broadcast_select_fusion = (f32[32,3,4,2048]{3,2,1,0:T(4,128)S(1)}, f32[32,3,4,2048]{3,2,1,0:T(4,128)}) fusion(f32[32,3,4,2048]{3,2,1,0:T(4,128)} %bitcast.116, pred[32,3]{1,0:T(8,128)(4,1)S(1)} %copy.122, f32[32,3,4,2048]{3,2,1,0:T(4,128)} %bitcast.117), kind=kLoop, calls=%fused_computation.23 | loop fusion | flops 1572864 | bytes 12583008 | tf_op jit(solution)/shard_map/jit(_take)/select_n | solution.py:18
  92.0 78.5 %all_to_all.115 = f32[32,3,4,2048]{3,2,1,0:T(4,128)} all-to-all(f32[32,3,4,2048]{3,2,1,0:T(4,128)S(1)} %get-tuple-element.31), channel_id=1, replica_groups=mesh['dp'=8,'seq'=32] {'seq'}, dimensions={0} | all-to-all | bytes 6291456 | tf_op jit(solution)/shard_map/all_to_all | solution.py:21
  170.4 8.4 %all-to-all-start.1 = ((f32[32,3,4,2048]{3,2,1,0:T(4,128)}), f32[32,3,4,2048]{3,2,1,0:T(4,128)S(1)}, u32[]{:S(2)}, u32[]{:S(2)}) async-start(f32[32,3,4,2048]{3,2,1,0:T(4,128)} %get-tuple-element.32), calls=%async_computation.1 | async-start | bytes 6291456 | tf_op jit(solution)/shard_map/all_to_all | solution.py:22
  178.9 2.9 broadcast_in_dim_reshape_squeeze.7
  181.8 2.5 copy.162
  186.7 6.9 %copy.131 = f32[1,3,32,4,2048]{4,0,3,2,1:T(1,128)} copy(f32[1,3,32,4,2048]{4,3,1,2,0:T(4,128)} %bitcast.115) | data formatting | bytes 6291456 | tf_op jit(solution)/shard_map/all_to_all | solution.py:21
  193.6 8.2 %pad_maximum_fusion.1 = f32[1,4,128,2048]{3,0,2,1:T(1,128)} fusion(f32[1,3,128,2048]{3,0,2,1:T(1,128)} %bitcast.118, f32[1,1,128,2048]{3,0,2,1:T(1,128)} %broadcast_in_dim_reshape_squeeze.7), kind=kLoop, calls=%fused_computation.4 | loop fusion | flops 1048576 | bytes 8388608 | tf_op jit(solution)/shard_map/concatenate | solution.py:75
  201.8 5.3 copy.138
  207.1 7.7 %fusion.22 = f32[16,128,512]{2,1,0:T(8,128)S(1)} fusion(f32[512,16,128]{0,2,1:T(8,128)} %copy.138, f32[128,16,128]{0,2,1:T(8,128)} %bitcast.120, f32[16]{0:T(128)S(1)} %broadcast_multiply_fusion), kind=kOutput, calls=%fused_computation.35 | convolution fusion | flops 1610874880 | bytes 9437248 | tf_op jit(solution)/shard_map/lqhd,lkhd->lhqk/dot_general | solution.py:85
  214.9 3.5 fusion.32
  218.4 7.0 %fusion.11 = f32[1,512,16,128]{3,1,2,0:T(8,128)S(1)} fusion(f32[16,128,512]{2,1,0:T(8,128)S(1)} %get-tuple-element.36, f32[16,128]{1,0:T(8,128)S(1)} %broadcast_divide_fusion, f32[128,16,128]{2,1,0:T(8,128)S(1)} %bitcast.122), kind=kOutput, calls=%fused_computation.19 | convolution fusion | flops 1611661312 | bytes 9445376 | tf_op jit(solution)/shard_map/lhqk,lqhd->lkhd/dot_general | solution.py:113
  225.5 2.4 copy.148
  229.9 2.7 slice.27
  232.6 4.1 copy.198
  236.7 15.4 %all-to-all-done.1 = f32[32,3,4,2048]{3,2,1,0:T(4,128)S(1)} async-done(((f32[32,3,4,2048]{3,2,1,0:T(4,128)}), f32[32,3,4,2048]{3,2,1,0:T(4,128)S(1)}, u32[]{:S(2)}, u32[]{:S(2)}) %all-to-all-start.1) | async-done | bytes 3145760 | tf_op jit(solution)/shard_map/all_to_all | solution.py:22
  252.1 5.8 all-to-all-start.6
  257.9 2.5 copy.136
  260.5 2.9 broadcast_in_dim_reshape_squeeze.6
  263.4 4.9 copy.125
  268.3 8.1 %pad_maximum_fusion = f32[1,4,128,2048]{3,0,2,1:T(1,128)} fusion(f32[1,3,128,2048]{3,0,2,1:T(1,128)} %bitcast.119, f32[1,1,128,2048]{3,0,2,1:T(1,128)} %broadcast_in_dim_reshape_squeeze.6), kind=kLoop, calls=%fused_computation.3 | loop fusion | flops 1048576 | bytes 8388608 | tf_op jit(solution)/shard_map/concatenate | solution.py:78
  276.4 5.8 copy.161
  282.2 7.8 %fusion.18 = (f32[128,16]{0,1:T(8,128)S(1)}, f32[16,128,128]{2,1,0:T(8,128)S(1)}) fusion(f32[1,128,16,128]{1,3,2,0:T(8,128)S(1)} %bitcast.125, f32[512,16,128]{0,2,1:T(8,128)} %copy.161, f32[16,128,512]{2,1,0:T(8,128)} %copy-done, f32[16,128]{1,0:T(8,128)S(1)} %broadcast_divide_fusion), kind=kOutput, calls=%fused_computation.31 | convolution fusion | flops 1612183552 | bytes 10502144 | tf_op jit(solution)/shard_map/lhqk,lkhd->lqhd/dot_general | solution.py:92
  290.0 6.8 %multiply_reduce_fusion = (f32[16]{0:T(128)S(1)}, f32[16,128,512]{2,1,0:T(8,128)S(1)}) fusion(f32[16,128,512]{2,1,0:T(8,128)S(1)} %copy-done.4, f32[16,128]{1,0:T(8,128)S(1)} %bitcast.128, f32[512,16,128]{0,2,1:T(8,128)} %copy.161, f32[128,16,128]{2,1,0:T(8,128)S(1)} %bitcast.123, f32[16,128,512]{2,1,0:T(8,128)S(1)} %copy-done.1, ...), kind=kOutput, calls=%fused_computation.7 | convolution fusion | flops 1615855616 | bytes 17842240 | tf_op jit(solution)/shard_map/lqhd,lkhd->lhqk/dot_general | solution.py:97
  298.8 5.3 convolution_bitcast_fusion
  304.0 5.3 reshape.172
  309.3 4.1 slice.25
  313.4 6.4 %copy.171 = f32[1,3,128,2048]{3,1,2,0:T(4,128)} copy(f32[1,3,128,2048]{2,1,3,0:T(4,128)} %slice.25) | data formatting | bytes 6291456
  319.8 34.8 %all-to-all-done.6 = f32[3,128,2048]{2,0,1:T(4,128)} async-done(((f32[3,128,2048]{2,0,1:T(4,128)}), f32[3,128,2048]{2,0,1:T(4,128)}, u32[]{:S(2)}, u32[]{:S(2)}) %all-to-all-start.6) | async-done | bytes 3145760 | tf_op jit(solution)/shard_map/all_to_all | solution.py:30
  354.6 6.9 %all-to-all-start.4 = ((f32[3,128,2048]{2,0,1:T(4,128)}), f32[3,128,2048]{2,0,1:T(4,128)}, u32[]{:S(2)}, u32[]{:S(2)}) async-start(f32[3,128,2048]{2,0,1:T(4,128)} %bitcast.109), calls=%async_computation.4 | async-start | bytes 8388608 | tf_op jit(solution)/shard_map/all_to_all | solution.py:29
  361.7 4.9 copy.150
  366.6 3.0 fusion.5
  371.2 87.0 %all-to-all-done.4 = f32[3,128,2048]{2,0,1:T(4,128)} async-done(((f32[3,128,2048]{2,0,1:T(4,128)}), f32[3,128,2048]{2,0,1:T(4,128)}, u32[]{:S(2)}, u32[]{:S(2)}) %all-to-all-start.4) | async-done | bytes 3145760 | tf_op jit(solution)/shard_map/all_to_all | solution.py:29
  458.2 6.7 %all-to-all-start.7 = ((f32[32,4,2048]{2,1,0:T(4,128)}), f32[32,4,2048]{2,1,0:T(4,128)S(1)}, u32[]{:S(2)}, u32[]{:S(2)}) async-start(f32[32,4,2048]{2,1,0:T(4,128)} %copy.152), calls=%async_computation.7 | async-start | bytes 2097152 | tf_op jit(solution)/shard_map/all_to_all | solution.py:48
  464.9 4.9 copy.143
  469.7 3.0 fusion.8
  474.4 15.2 %all-to-all-done.7 = f32[32,4,2048]{2,1,0:T(4,128)S(1)} async-done(((f32[32,4,2048]{2,1,0:T(4,128)}), f32[32,4,2048]{2,1,0:T(4,128)S(1)}, u32[]{:S(2)}, u32[]{:S(2)}) %all-to-all-start.7) | async-done | bytes 1048608 | tf_op jit(solution)/shard_map/all_to_all | solution.py:48
  489.5 8.4 %all-to-all-start.5 = ((f32[32,4,2048]{2,1,0:T(4,128)}), f32[32,4,2048]{2,1,0:T(4,128)}, u32[]{:S(2)}, u32[]{:S(2)}) async-start(f32[32,4,2048]{2,1,0:T(4,128)} %copy.145), calls=%async_computation.5 | async-start | bytes 2097152 | tf_op jit(solution)/shard_map/all_to_all | solution.py:47
  498.0 78.3 %psum.7 = f32[16]{0:T(128)} all-reduce(f32[16]{0:T(128)S(1)} %div.16), channel_id=1, replica_groups=mesh['dp'=8,'seq'=32] {'dp','seq'}, use_global_device_ids=true, to_apply=%region_4.6 | all-reduce | flops 16 | bytes 128 | tf_op jit(solution)/shard_map/psum | solution.py:125
  577.5 7.5 %fusion.16 = f32[1,16,128,128]{3,2,1,0:T(8,128)S(1)} fusion(f32[512,16,128]{0,2,1:T(8,128)} %copy.138, f32[16,128,512]{2,1,0:T(8,128)} %copy-done.2, f32[16]{0:T(128)S(1)} %broadcast_multiply_fusion), kind=kOutput, calls=%fused_computation.26 | convolution fusion | flops 1610874880 | bytes 9437248 | tf_op jit(solution)/shard_map/lhqk,lkhd->lqhd/dot_general | solution.py:107
  (54 shorter events, 23.8 us)
Async XLA Ops:
  0.6 15.4 %copy-start.10 = (f32[1,128,2048]{2,1,0:T(8,128)S(1)}, f32[1,128,2048]{2,1,0:T(8,128)}, u32[]{:S(2)}) copy-start(f32[1,128,2048]{2,1,0:T(8,128)} %param.10) | copy-start | bytes 3145732
  0.6 48.8 %copy-start.11 = (s32[1,32,4]{1,2,0:T(4,128)S(1)}, s32[1,32,4]{1,2,0:T(4,128)}, u32[]{:S(2)}) copy-start(s32[1,32,4]{1,2,0:T(4,128)} %param.12) | copy-start | bytes 1540
  4.0 36.7 %all-to-all-start.2 = ((f32[1,128,2048]{2,0,1:T(1,128)}), f32[1,128,2048]{2,0,1:T(1,128)S(1)}, u32[]{:S(2)}, u32[]{:S(2)}) async-start(f32[1,128,2048]{2,0,1:T(1,128)} %copy.129), calls=%async_computation.2 | async-start | bytes 2097152 | tf_op jit(solution)/shard_map/all_to_all | solution.py:15
  40.7 33.5 %all-to-all-start = ((f32[1,128,2048]{2,0,1:T(1,128)}), f32[1,128,2048]{2,0,1:T(1,128)S(1)}, u32[]{:S(2)}, u32[]{:S(2)}) async-start(f32[1,128,2048]{2,0,1:T(1,128)} %copy.123), calls=%async_computation | async-start | bytes 2097152 | tf_op jit(solution)/shard_map/all_to_all | solution.py:16
  170.4 81.7 %all-to-all-start.1 = ((f32[32,3,4,2048]{3,2,1,0:T(4,128)}), f32[32,3,4,2048]{3,2,1,0:T(4,128)S(1)}, u32[]{:S(2)}, u32[]{:S(2)}) async-start(f32[32,3,4,2048]{3,2,1,0:T(4,128)} %get-tuple-element.32), calls=%async_computation.1 | async-start | bytes 6291456 | tf_op jit(solution)/shard_map/all_to_all | solution.py:22
  178.9 7.8 %copy-start.12 = (f32[16]{0:T(128)S(1)}, f32[16]{0:T(128)}, u32[]{:S(2)}) copy-start(f32[16]{0:T(128)} %param.11) | copy-start | bytes 196
  214.9 3.5 copy-start.3
  214.9 3.5 copy-start.7
  218.4 7.1 %copy-start = (f32[16,128,512]{2,1,0:T(8,128)}, f32[16,128,512]{2,1,0:T(8,128)S(1)}, u32[]{:S(2)}) copy-start(f32[16,128,512]{2,1,0:T(8,128)S(1)} %get-tuple-element.36) | copy-start | bytes 12582916
  227.9 2.0 copy-start.5
  252.1 102.4 %all-to-all-start.6 = ((f32[3,128,2048]{2,0,1:T(4,128)}), f32[3,128,2048]{2,0,1:T(4,128)}, u32[]{:S(2)}, u32[]{:S(2)}) async-start(f32[3,128,2048]{2,0,1:T(4,128)} %bitcast.108), calls=%async_computation.6 | async-start | bytes 8388608 | tf_op jit(solution)/shard_map/all_to_all | solution.py:30
  276.4 5.8 copy-start.9
  282.2 7.8 %copy-start.1 = (f32[16,128,512]{2,1,0:T(8,128)S(1)}, f32[16,128,512]{2,1,0:T(8,128)}, u32[]{:S(2)}) copy-start(f32[16,128,512]{2,1,0:T(8,128)} %copy-done) | copy-start | bytes 12582916
  282.2 7.8 %copy-start.4 = (f32[16,128,512]{2,1,0:T(8,128)S(1)}, f32[16,128,512]{2,1,0:T(8,128)}, u32[]{:S(2)}) copy-start(f32[16,128,512]{2,1,0:T(8,128)} %copy-done.3) | copy-start | bytes 12582916
  282.2 7.8 %copy-start.8 = (f32[16,8,16,128]{3,2,1,0:T(8,128)S(1)}, f32[16,8,16,128]{3,2,1,0:T(8,128)}, u32[]{:S(2)}) copy-start(f32[16,8,16,128]{3,2,1,0:T(8,128)} %copy.174) | copy-start | bytes 3145732
  290.0 8.7 %copy-start.6 = (f32[1,128,2048]{1,2,0:T(8,128)S(1)}, f32[1,128,2048]{1,2,0:T(8,128)}, u32[]{:S(2)}) copy-start(f32[1,128,2048]{1,2,0:T(8,128)} %copy.162) | copy-start | bytes 3145732
  296.8 1.9 copy-start.2
  354.6 103.6 %all-to-all-start.4 = ((f32[3,128,2048]{2,0,1:T(4,128)}), f32[3,128,2048]{2,0,1:T(4,128)}, u32[]{:S(2)}, u32[]{:S(2)}) async-start(f32[3,128,2048]{2,0,1:T(4,128)} %bitcast.109), calls=%async_computation.4 | async-start | bytes 8388608 | tf_op jit(solution)/shard_map/all_to_all | solution.py:29
  458.2 31.3 %all-to-all-start.7 = ((f32[32,4,2048]{2,1,0:T(4,128)}), f32[32,4,2048]{2,1,0:T(4,128)S(1)}, u32[]{:S(2)}, u32[]{:S(2)}) async-start(f32[32,4,2048]{2,1,0:T(4,128)} %copy.152), calls=%async_computation.7 | async-start | bytes 2097152 | tf_op jit(solution)/shard_map/all_to_all | solution.py:48
  489.5 102.5 %all-to-all-start.5 = ((f32[32,4,2048]{2,1,0:T(4,128)}), f32[32,4,2048]{2,1,0:T(4,128)}, u32[]{:S(2)}, u32[]{:S(2)}) async-start(f32[32,4,2048]{2,1,0:T(4,128)} %copy.145), calls=%async_computation.5 | async-start | bytes 2097152 | tf_op jit(solution)/shard_map/all_to_all | solution.py:47
  577.5 8.8 %slice-start = ((f32[1,4,128,2048]{2,1,3,0:T(4,128)}), f32[1,1,128,2048]{2,1,3,0:T(1,128)S(1)}, s32[]{:S(2)}) async-start(f32[1,4,128,2048]{2,1,3,0:T(4,128)} %reshape.172), calls=%async_computation.8 | async-start | bytes 2097152 | tf_op jit(solution)/shard_map/slice | solution.py:118
where the time goes:
time: 599 us; the launch traced here: 595 us
  waiting for transfers between devices  197 us (33%)
  blocking collectives  157 us (26%)
  local copies, waits for them, and re-layouts  100 us (17%)
  starting transfers between devices  57 us (10%)
  matrix products  48 us (8%)
  other arithmetic  35 us (6%)
    all_to_all x1, waiting for transfers between devices, return_listed(): lax.all_to_all(key_terms, 'seq', split_axis=1, concat_axis=0, tiled=True)  87 us
    all_to_all x1, blocking collectives, fetch_listed(): lax.all_to_all(key_send, 'seq', split_axis=0, concat_axis=2, tiled=True)  78.5 us
    psum x1, blocking collectives, per_device(): lax.psum(sharpness_contributions, ('dp', 'seq'))  78.3 us
    all_to_all x1, waiting for transfers between devices, return_listed(): lax.all_to_all(value_terms, 'seq', split_axis=1, concat_axis=0, tiled=True)  34.8 us
    unnamed x35, local copies, waits for them, and re-layouts  25.3 us
    all_to_all x1, waiting for transfers between devices, fetch_listed(): lax.all_to_all(key_blocks, 'seq', split_axis=1, concat_axis=0, tiled=True)  22.6 us
    all_to_all x1, waiting for transfers between devices, fetch_listed(): lax.all_to_all(value_blocks, 'seq', split_axis=1, concat_axis=0, tiled=True)  21.6 us
    all_to_all x1, waiting for transfers between devices, fetch_listed(): lax.all_to_all(value_send, 'seq', split_axis=0, concat_axis=2, tiled=True)  15.4 us
  transfers between devices with their start and end apart: 7, of which 6 were waited for; matrix products, arithmetic and copies ran while one was open for 26% of the time, Pallas kernels for 0%

commit v1 on v0

v1 whole, which is shorter than its diff:
```python
import functools
import math

import jax
import jax.numpy as jnp
from jax import lax
from jax.experimental import pallas as pl
from jax.experimental.pallas import tpu as pltpu
from jax.sharding import PartitionSpec as P

HD = 128
BLOCK = 128
NB = 4
MESH = pl.DeviceIdType.MESH
HIGH = lax.Precision.HIGHEST


def dot(a, b, ca, cb):
    return lax.dot_general(
        a, b, (((ca,), (cb,)), ((), ())), precision=HIGH, preferred_element_type=jnp.float32
    )


def kernel(
    chips,
    dps,
    q_ref,
    k_ref,
    v_ref,
    g_ref,
    adj_ref,
    sharp_ref,
    o_ref,
    dq_ref,
    dk_ref,
    dv_ref,
    ds_ref,
    kx,
    vx,
    qg,
    oq,
    dk,
    dv,
    runk,
    runv,
    part,
    adjv,
    adjs,
    prevs,
    lasts,
    sh_own,
    sh_sib,
    sh_tot,
    sh_all,
    dp_all,
    send_in,
    send_relay,
    send_oq,
    send_dkv,
    send_part,
    send_small,
    recv_kv,
    recv_q,
    recv_relay,
    recv_part,
    recv_out,
    recv_small,
):
    heads = chips // 2
    dp = lax.axis_index("dp")
    c = lax.axis_index("seq")
    X2 = (dp // 2) * 2
    s = dp % 2
    p = c % 2
    head = c // 2
    same = p == s
    sibling = (X2 + 1 - s, c)

    def partner(i):
        return (X2 + p, 2 * i + s)

    def is_self(i):
        return jnp.logical_and(same, 2 * i + s == c)

    barrier = pltpu.get_barrier_semaphore()

    def greet(i, _):
        @pl.when(jnp.logical_not(is_self(i)))
        def _():
            pl.semaphore_signal(barrier, inc=1, device_id=partner(i), device_id_type=MESH)

        return _

    lax.fori_loop(0, heads, greet, None)

    def greet_dp(i, _):
        @pl.when(i != dp)
        def _():
            pl.semaphore_signal(barrier, inc=1, device_id=(i, c), device_id_type=MESH)

        return _

    lax.fori_loop(0, dps, greet_dp, None)
    pl.semaphore_wait(barrier, jnp.where(same, heads - 1, heads) + dps - 1)

    def put(i, src, dst, send, recv):
        @pl.when(is_self(i))
        def _():
            pltpu.make_async_copy(src, dst, recv).start()

        @pl.when(jnp.logical_not(is_self(i)))
        def _():
            pltpu.make_async_remote_copy(
                src, dst, send, recv, device_id=partner(i), device_id_type=MESH
            ).start()

    def columns(ref, h):
        return ref.at[:, pl.ds(pl.multiple_of(h * HD, HD), HD)]

    def to_sibling(src, dst, send, recv):
        return pltpu.make_async_remote_copy(
            src, dst, send, recv, device_id=sibling, device_id_type=MESH
        )

    adj_copy = to_sibling(adj_ref, adjv.at[1], send_small.at[0], recv_small.at[0])
    adj_copy.start()
    own_adj = pltpu.make_async_copy(adj_ref, adjv.at[0], recv_small.at[1])
    own_adj.start()

    def send_k(t, _):
        h = lax.rem(head + t, heads)
        put(h, columns(k_ref, h), kx.at[p, head], send_in, recv_kv.at[0])
        return _

    def send_v(t, _):
        h = lax.rem(head + t, heads)
        put(h, columns(v_ref, h), vx.at[p, head], send_in, recv_kv.at[1])
        return _

    def send_q(t, _):
        h = lax.rem(head + t, heads)
        put(h, columns(q_ref, h), qg.at[head, 0], send_in, recv_q.at[head])
        put(h, columns(g_ref, h), qg.at[head, 1], send_in, recv_q.at[head])
        return _

    lax.fori_loop(0, heads, send_k, None)
    lax.fori_loop(0, heads, send_v, None)
    lax.fori_loop(0, heads, send_q, None)

    adj_copy.wait()
    own_adj.wait()
    to_scalars = pltpu.make_async_copy(adjv.at[jnp.where(same, 0, 1)], adjs, recv_small.at[1])
    to_scalars.start()
    to_scalars.wait()

    def slot_of(t):
        return lax.rem(head - t + heads, heads)

    def far_of(t):
        return adjs[0, (2 * slot_of(t) + s) * NB + NB - 1]

    def chain(t, _):
        mine = far_of(t)

        def look(u, found):
            return jnp.where(jnp.logical_and(u < t, far_of(u) == mine), u, found)

        prevs[t] = lax.fori_loop(0, heads, look, jnp.int32(-1))
        return _

    lax.fori_loop(0, heads, chain, None)

    def last_of(k, _):
        def look(u, found):
            return jnp.where(far_of(u) == k, u, found)

        lasts[k] = lax.fori_loop(0, heads, look, jnp.int32(-1))
        return _

    lax.fori_loop(0, chips, last_of, None)

    def clear(i, _):
        dk[0, i, :, :] = jnp.zeros((BLOCK, HD), jnp.float32)
        dk[1, i, :, :] = jnp.zeros((BLOCK, HD), jnp.float32)
        dv[0, i, :, :] = jnp.zeros((BLOCK, HD), jnp.float32)
        dv[1, i, :, :] = jnp.zeros((BLOCK, HD), jnp.float32)
        return _

    lax.fori_loop(0, heads, clear, None)

    for i, ref in enumerate((kx, vx)):
        pltpu.make_async_copy(ref.at[s], ref.at[s], recv_kv.at[i]).wait()
        to_sibling(ref.at[s], ref.at[s], send_relay.at[i], recv_relay.at[i]).start()
    for i, ref in enumerate((kx, vx)):
        pltpu.make_async_copy(ref.at[1 - s], ref.at[1 - s], recv_relay.at[i]).wait()

    sharp = sharp_ref[head]
    scale = sharp * (1.0 / math.sqrt(HD))

    def step(t, acc):
        j = slot_of(t)
        b = 2 * j + s
        pltpu.make_async_copy(qg.at[j], qg.at[j], recv_q.at[j]).wait()
        q = qg[j, 0] * scale
        g = qg[j, 1]
        far = far_of(t)
        before = lax.rem(b + chips - 1, chips)
        after = lax.rem(b + 1, chips)

        def listed(ref):
            return jnp.concatenate(
                [ref[s, j], ref[1 - s, before // 2], ref[1 - s, after // 2], ref[far % 2, far // 2]],
                axis=0,
            )

        keys = listed(kx)
        values = listed(vx)
        logits = dot(keys, q, 1, 1)
        prob_grad = dot(values, g, 1, 1)
        top = jnp.max(logits, axis=0, keepdims=True)
        shifted = jnp.exp(logits - top)
        prob = shifted * (1.0 / jnp.sum(shifted, axis=0, keepdims=True))
        row_dot = jnp.sum(prob * prob_grad, axis=0, keepdims=True)
        score_grad = prob * (prob_grad - row_dot)
        acc = acc + jnp.sum(score_grad * logits, axis=0, keepdims=True)
        oq[j, 0] = dot(prob, values, 0, 0)
        oq[j, 1] = dot(score_grad, keys, 0, 0) * scale
        put(j, oq.at[j, 0], columns(o_ref, head), send_oq, recv_out.at[0])
        put(j, oq.at[j, 1], columns(dq_ref, head), send_oq, recv_out.at[1])
        key_terms = dot(score_grad, q, 1, 0)
        value_terms = dot(prob, g, 1, 0)
        back = prevs[t]
        at = jnp.maximum(back, 0)
        for total, run, terms in ((dk, runk, key_terms), (dv, runv, value_terms)):
            total[s, j] += terms[:BLOCK]
            total[1 - s, before // 2] += terms[BLOCK : 2 * BLOCK]
            total[1 - s, after // 2] += terms[2 * BLOCK : 3 * BLOCK]
            run[t] = terms[3 * BLOCK :] + jnp.where(back >= 0, run[at], 0.0)
        return acc

    acc = lax.fori_loop(0, heads, step, jnp.zeros((1, HD), jnp.float32))

    sh_own[...] = jnp.broadcast_to(jnp.sum(acc, axis=1, keepdims=True) / sharp, (8, HD))
    small = to_sibling(sh_own, sh_sib, send_small.at[1], recv_small.at[2])
    small.start()

    def gather(total, run, half, i):
        at = lasts[2 * i + half]
        return total[half, i] + jnp.where(at >= 0, run[jnp.maximum(at, 0)], 0.0)

    def far_sibling(i, _):
        dk[1 - s, i] = gather(dk, runk, 1 - s, i)
        dv[1 - s, i] = gather(dv, runv, 1 - s, i)
        return _

    lax.fori_loop(0, heads, far_sibling, None)
    for i, ref in enumerate((dk, dv)):
        to_sibling(ref.at[1 - s], part.at[i], send_part.at[i], recv_part.at[i]).start()

    small.wait()
    sh_tot[...] = sh_own[...] + sh_sib[...]

    def send_sharp(i, _):
        put(i, sh_tot, sh_all.at[head], send_small.at[2], recv_small.at[3])
        return _

    lax.fori_loop(0, heads, send_sharp, None)

    for i in range(2):
        pltpu.make_async_copy(part.at[i], part.at[i], recv_part.at[i]).wait()

    def finish(t, _):
        j = slot_of(t)
        dk[s, j] = gather(dk, runk, s, j) + part[0, j]
        dv[s, j] = gather(dv, runv, s, j) + part[1, j]
        put(j, dk.at[s, j], columns(dk_ref, head), send_dkv, recv_out.at[2])
        put(j, dv.at[s, j], columns(dv_ref, head), send_dkv, recv_out.at[3])
        return _

    lax.fori_loop(0, heads, finish, None)

    pltpu.make_async_copy(sh_all, sh_all, recv_small.at[3]).wait()
    dp_all[dp] = sh_all[:, 0, :]

    def send_dp(i, _):
        @pl.when(i != dp)
        def _():
            pltpu.make_async_remote_copy(
                dp_all.at[dp],
                dp_all.at[dp],
                send_small.at[3],
                recv_small.at[4],
                device_id=(i, c),
                device_id_type=MESH,
            ).start()

        return _

    lax.fori_loop(0, dps, send_dp, None)
    others = dp_all.at[pl.ds(0, dps - 1)]
    pltpu.make_async_copy(others, others, recv_small.at[4]).wait()
    total = dp_all[0]
    for i in range(1, dps):
        total = total + dp_all[i]
    ds_ref[...] = total

    pltpu.make_async_copy(others, others, send_small.at[3]).wait()
    for i, ref in enumerate((kx, vx)):
        pltpu.make_async_copy(ref.at[s], ref.at[s], send_relay.at[i]).wait()
    for i in range(2):
        pltpu.make_async_copy(part.at[i], part.at[i], send_part.at[i]).wait()

    def drain(count):
        few = qg.at[pl.ds(0, count)]
        pltpu.make_async_copy(few, few, send_in).wait()
        pltpu.make_async_copy(few, few, send_in).wait()
        pltpu.make_async_copy(few, few, send_oq).wait()
        pltpu.make_async_copy(few, few, send_dkv).wait()
        tiles = sh_all.at[pl.ds(0, count)]
        pltpu.make_async_copy(tiles, tiles, send_small.at[2]).wait()

    @pl.when(same)
    def _():
        drain(heads - 1)

    @pl.when(jnp.logical_not(same))
    def _():
        drain(heads)

    for i, ref in enumerate((o_ref, dq_ref, dk_ref, dv_ref)):
        pltpu.make_async_copy(ref, ref, recv_out.at[i]).wait()


def per_device(queries, keys, values, sharpness, listing, adjoint):
    chips = lax.axis_size("seq")
    dps = lax.axis_size("dp")
    heads = chips // 2
    rows, features = queries.shape[1:]
    f32 = jnp.float32
    anywhere = pl.BlockSpec(memory_space=pl.ANY)
    block = (BLOCK, HD)
    whole = jax.ShapeDtypeStruct((rows, features), f32)
    dma = pltpu.SemaphoreType.DMA
    o, dq, dk, dv, ds = pl.pallas_call(
        functools.partial(kernel, chips, dps),
        out_shape=[whole] * 4 + [jax.ShapeDtypeStruct((heads, HD), f32)],
        in_specs=[anywhere] * 5 + [pl.BlockSpec(memory_space=pltpu.SMEM)],
        out_specs=[anywhere] * 4 + [pl.BlockSpec(memory_space=pltpu.VMEM)],
        scratch_shapes=[
            pltpu.VMEM((2, heads) + block, f32),
            pltpu.VMEM((2, heads) + block, f32),
            pltpu.VMEM((heads, 2) + block, f32),
            pltpu.VMEM((heads, 2) + block, f32),
            pltpu.VMEM((2, heads) + block, f32),
            pltpu.VMEM((2, heads) + block, f32),
            pltpu.VMEM((heads,) + block, f32),
            pltpu.VMEM((heads,) + block, f32),
            pltpu.VMEM((2, heads) + block, f32),
            pltpu.VMEM((2, 1, chips * NB), jnp.int32),
            pltpu.SMEM((1, chips * NB), jnp.int32),
            pltpu.SMEM((heads,), jnp.int32),
            pltpu.SMEM((chips,), jnp.int32),
            pltpu.VMEM((8, HD), f32),
            pltpu.VMEM((8, HD), f32),
            pltpu.VMEM((8, HD), f32),
            pltpu.VMEM((heads, 8, HD), f32),
            pltpu.VMEM((dps, heads, HD), f32),
            dma,
            dma((2,)),
            dma,
            dma,
            dma((2,)),
            dma((4,)),
            dma((2,)),
            dma((heads,)),
            dma((2,)),
            dma((2,)),
            dma((4,)),
            dma((5,)),
        ],
        compiler_params=pltpu.CompilerParams(
            collective_id=0, has_side_effects=True, vmem_limit_bytes=48 * 2**20
        ),
        name="attend",
    )(
        queries[0],
        keys[0],
        values[0],
        adjoint[0],
        listing.reshape(1, chips * NB),
        sharpness,
    )
    return o[None], dq[None], dk[None], dv[None], ds[:, 0]


def solution(mesh):
    tokens = P("dp", "seq", None)
    return jax.shard_map(
        per_device,
        mesh=mesh,
        in_specs=(tokens, tokens, tokens, P(), P("dp", None, None), tokens),
        out_specs=(tokens, tokens, tokens, tokens, P()),
        check_vma=False,
    )
```

time: 599 us -> 204 us (0.34)
  waiting for transfers between devices: 197 us -> 0 us
  Pallas kernels: 0 us -> 196 us
  blocking collectives: 157 us -> 0 us
  local copies, waits for them, and re-layouts: 100 us -> 7.14 us
  starting transfers between devices: 57 us -> 0 us
  matrix products: 48 us -> 0 us
  other arithmetic: 35 us -> 0 us
    all_to_all x7 -> x0, waiting for transfers between devices: 197 us -> none  [the longest x1 87 us: return_listed(): lax.all_to_all(key_terms, 'seq', split_axis=1, concat_axis=0, tiled=True)]
    pallas_call x0 -> x1, Pallas kernels: none -> 196 us  [per_device(): pl.pallas_call(functools.partial(kernel, chips, dps), out_shape=[whole] *...]
    all_to_all x1 -> x0, blocking collectives: 78.5 us -> none  [fetch_listed(): lax.all_to_all(key_send, 'seq', split_axis=0, concat_axis=2, tiled=True)]
    psum x1 -> x0, blocking collectives: 78.3 us -> none  [per_device(): lax.psum(sharpness_contributions, ('dp', 'seq'))]
    all_to_all x7 -> x0, starting transfers between devices: 57 us -> none  [the longest x1 12 us: fetch_listed(): lax.all_to_all(key_blocks, 'seq', split_axis=1, concat_axis=0, tiled=True)]
    dot_general x8 -> x0, matrix products: 48 us -> none  [the longest x1 7.76 us: per_device(): jnp.einsum('lhqk,lkhd->lqhd', normalized_probabilities, listed_value, pre...]
    all_to_all x8 -> x0, local copies, waits for them, and re-layouts: 25.2 us -> none  [the longest x1 6.93 us: fetch_listed(): lax.all_to_all(key_send, 'seq', split_axis=0, concat_axis=2, tiled=True)]
    another operation x5 -> x0, local copies, waits for them, and re-layouts: 19.4 us -> none
  transfers between devices with their start and end apart: 7 -> 0, of which waited for: 6 -> 0; matrix products, arithmetic and copies ran while one was open for 26% -> 0% of each run, Pallas kernels for 0% -> 0%
where the time goes in v1:
time: 204 us
  Pallas kernels  196 us (96%)
  local copies, waits for them, and re-layouts  7.14 us (4%)
    pallas_call x1, Pallas kernels, per_device(): pl.pallas_call(functools.partial(kernel, chips, dps), out_shape=[whole] *...  196 us
    unnamed x11, local copies, waits for them, and re-layouts  6.41 us

profile of v1, /device:TPU:1, one launch (start us, length us, event | category | flops | bytes accessed | tf_op | source)
XLA Modules:
  0.0 204.1 jit_solution(17702615542027958993)
XLA Ops:
  0.6 0.0 copy-start.2
  0.6 0.7 copy-done.2
  1.3 0.1 copy.12
  1.4 0.0 copy-start.1
  1.4 0.1 reshape.13.adj_ref
  1.5 0.5 copy-done.1
  2.1 0.0 copy-start
  2.1 1.2 copy-done
  3.3 196.3 %attend.1 = (f32[128,2048]{1,0:T(8,128)S(1)}, f32[128,2048]{1,0:T(8,128)S(1)}, f32[128,2048]{1,0:T(8,128)S(1)}, f32[128,2048]{1,0:T(8,128)S(1)}, f32[16,128]{1,0:T(8,128)S(1)}) custom-call(f32[128,2048]{1,0:T(8,128)S(1)} %bitcast.8, f32[128,2048]{1,0:T(8,128)} %bitcast.13, f32[128,2048]{1,0:T(8,128)} %bitcast.14, f32[128,2048]{1,0:T(8,128)} %bitcast.15, ...), custom_call_target="tpu_custom_call" | custom-call | tf_op jit(solution)/shard_map/attend/pallas_call | solution.py:344
  199.6 0.6 slice_reduce_fusion
  200.2 1.0 copy.17
  201.2 1.0 copy.18
  202.2 1.0 copy.19
  203.1 1.0 copy.20
Async XLA Ops:
  0.6 0.7 copy-start.2
  1.4 0.7 copy-start.1
  2.1 1.2 copy-start

commit v2 on v1

--- a/solution.py
+++ b/solution.py
@@ -46,6 +46,7 @@
     part,
     adjv,
     adjs,
+    sharps,
     prevs,
     lasts,
     sh_own,
@@ -126,6 +127,8 @@
     adj_copy.start()
     own_adj = pltpu.make_async_copy(adj_ref, adjv.at[0], recv_small.at[1])
     own_adj.start()
+    own_sharp = pltpu.make_async_copy(sharp_ref, sharps, recv_small.at[5])
+    own_sharp.start()
 
     def send_k(t, _):
         h = lax.rem(head + t, heads)
@@ -149,6 +152,7 @@
 
     adj_copy.wait()
     own_adj.wait()
+    own_sharp.wait()
     to_scalars = pltpu.make_async_copy(adjv.at[jnp.where(same, 0, 1)], adjs, recv_small.at[1])
     to_scalars.start()
     to_scalars.wait()
@@ -157,7 +161,7 @@
         return lax.rem(head - t + heads, heads)
 
     def far_of(t):
-        return adjs[0, (2 * slot_of(t) + s) * NB + NB - 1]
+        return adjs[NB - 1, 2 * slot_of(t) + s]
 
     def chain(t, _):
         mine = far_of(t)
@@ -194,7 +198,7 @@
     for i, ref in enumerate((kx, vx)):
         pltpu.make_async_copy(ref.at[1 - s], ref.at[1 - s], recv_relay.at[i]).wait()
 
-    sharp = sharp_ref[head]
+    sharp = sharps[head]
     scale = sharp * (1.0 / math.sqrt(HD))
 
     def step(t, acc):
@@ -302,7 +306,9 @@
     total = dp_all[0]
     for i in range(1, dps):
         total = total + dp_all[i]
-    ds_ref[...] = total
+    lane = lax.broadcasted_iota(jnp.int32, total.shape, 1)
+    row = lax.broadcasted_iota(jnp.int32, total.shape, 0)
+    ds_ref[...] = jnp.sum(jnp.where(lane == row, total, 0.0), axis=0, keepdims=True)[:, :heads]
 
     pltpu.make_async_copy(others, others, send_small.at[3]).wait()
     for i, ref in enumerate((kx, vx)):
@@ -329,6 +335,33 @@
 
     for i, ref in enumerate((o_ref, dq_ref, dk_ref, dv_ref)):
         pltpu.make_async_copy(ref, ref, recv_out.at[i]).wait()
+
+
+def settle_kernel(*refs):
+    ins, outs, sems = refs[:4], refs[4:8], refs[8]
+    pieces = sems.shape[1]
+    copies = []
+    for a, (src, dst) in enumerate(zip(ins, outs)):
+        rows = src.shape[0] // pieces
+        for i in range(pieces):
+            part = pl.ds(i * rows, rows)
+            copies.append(pltpu.make_async_copy(src.at[part], dst.at[part], sems.at[a, i]))
+    for copy in copies:
+        copy.start()
+    for copy in copies:
+        copy.wait()
+
+
+def settle(*arrays):
+    anywhere = pl.BlockSpec(memory_space=pl.ANY)
+    return pl.pallas_call(
+        settle_kernel,
+        out_shape=[jax.ShapeDtypeStruct(x.shape, x.dtype) for x in arrays],
+        in_specs=[anywhere] * 4,
+        out_specs=[pl.BlockSpec(memory_space=pltpu.HBM)] * 4,
+        scratch_shapes=[pltpu.SemaphoreType.DMA((4, 2))],
+        name="settle",
+    )(*arrays)
 
 
 def per_device(queries, keys, values, sharpness, listing, adjoint):
@@ -343,8 +376,8 @@
     dma = pltpu.SemaphoreType.DMA
     o, dq, dk, dv, ds = pl.pallas_call(
         functools.partial(kernel, chips, dps),
-        out_shape=[whole] * 4 + [jax.ShapeDtypeStruct((heads, HD), f32)],
-        in_specs=[anywhere] * 5 + [pl.BlockSpec(memory_space=pltpu.SMEM)],
+        out_shape=[whole] * 4 + [jax.ShapeDtypeStruct((1, heads), f32)],
+        in_specs=[pl.BlockSpec(memory_space=pltpu.HBM)] * 6,
         out_specs=[anywhere] * 4 + [pl.BlockSpec(memory_space=pltpu.VMEM)],
         scratch_shapes=[
             pltpu.VMEM((2, heads) + block, f32),
@@ -356,8 +389,9 @@
             pltpu.VMEM((heads,) + block, f32),
             pltpu.VMEM((heads,) + block, f32),
             pltpu.VMEM((2, heads) + block, f32),
-            pltpu.VMEM((2, 1, chips * NB), jnp.int32),
-            pltpu.SMEM((1, chips * NB), jnp.int32),
+            pltpu.VMEM((2, NB, chips), jnp.int32),
+            pltpu.SMEM((NB, chips), jnp.int32),
+            pltpu.SMEM((heads,), f32),
             pltpu.SMEM((heads,), jnp.int32),
             pltpu.SMEM((chips,), jnp.int32),
             pltpu.VMEM((8, HD), f32),
@@ -376,21 +410,20 @@
             dma((2,)),
             dma((2,)),
             dma((4,)),
-            dma((5,)),
+            dma((6,)),
         ],
         compiler_params=pltpu.CompilerParams(
             collective_id=0, has_side_effects=True, vmem_limit_bytes=48 * 2**20
         ),
         name="attend",
     )(
-        queries[0],
-        keys[0],
-        values[0],
-        adjoint[0],
-        listing.reshape(1, chips * NB),
-        sharpness,
+        *(
+            pltpu.with_memory_space_constraint(x, pltpu.HBM)
+            for x in (queries[0], keys[0], values[0], adjoint[0], listing[0].T, sharpness)
+        )
     )
-    return o[None], dq[None], dk[None], dv[None], ds[:, 0]
+    o, dq, dk, dv = settle(o, dq, dk, dv)
+    return o[None], dq[None], dk[None], dv[None], ds[0]
 
 
 def solution(mesh):

time: 204 us -> 329 us (1.61)
  Pallas kernels: 196 us -> 324 us
    pallas_call x0 -> x1, Pallas kernels: none -> 128 us  [settle(): pl.pallas_call(settle_kernel, out_shape=[jax.ShapeDtypeStruct(x.shape, x....]
where the time goes in v2:
time: 329 us
  Pallas kernels  324 us (98%)
  local copies, waits for them, and re-layouts  4.46 us (1%)
    pallas_call x1, Pallas kernels, per_device(): pl.pallas_call(functools.partial(kernel, chips, dps), out_shape=[whole] *...  196 us
    pallas_call x1, Pallas kernels, settle(): pl.pallas_call(settle_kernel, out_shape=[jax.ShapeDtypeStruct(x.shape, x....  128 us

profile of v2, /device:TPU:1, one launch (start us, length us, event | category | flops | bytes accessed | tf_op | source)
XLA Modules:
  0.0 329.3 jit_solution(17973584908449316900)
XLA Ops:
  0.6 195.9 %attend.1 = (f32[128,2048]{1,0:T(8,128)S(1)}, f32[128,2048]{1,0:T(8,128)S(1)}, f32[128,2048]{1,0:T(8,128)S(1)}, f32[128,2048]{1,0:T(8,128)S(1)}, f32[1,16]{1,0:T(1,128)S(1)}) custom-call(f32[128,2048]{1,0:T(8,128)} %bitcast.13, f32[128,2048]{1,0:T(8,128)} %bitcast.14, f32[128,2048]{1,0:T(8,128)} %bitcast.15, f32[128,2048]{1,0:T(8,128)} %bitcast.16, ...), custom_call_target="tpu_custom_call" | custom-call | tf_op jit(solution)/shard_map/attend/pallas_call | solution.py:377
  196.5 0.0 copy-start
  196.6 1.0 copy-done
  197.5 0.0 copy-start.1
  197.5 1.0 copy-done.1
  198.5 0.0 copy-start.2
  198.5 1.0 copy-done.2
  199.5 0.0 copy-start.3
  199.5 1.0 copy-done.3
  200.5 128.2 %settle.1 = (f32[128,2048]{1,0:T(8,128)}, f32[128,2048]{1,0:T(8,128)}, f32[128,2048]{1,0:T(8,128)}, f32[128,2048]{1,0:T(8,128)}) custom-call(f32[128,2048]{1,0:T(8,128)} %copy-done, f32[128,2048]{1,0:T(8,128)} %copy-done.1, f32[128,2048]{1,0:T(8,128)} %copy-done.2, f32[128,2048]{1,0:T(8,128)} %copy-done.3), custom_call_target="tpu_custom_call" | custom-call | tf_op jit(solution)/shard_map/settle/pallas_call | solution.py:357
  328.7 0.5 copy.12
Async XLA Ops:
  196.5 1.0 copy-start
  197.5 1.0 copy-start.1
  198.5 1.0 copy-start.2
  199.5 1.0 copy-start.3

commit v3 on v2

--- a/solution.py
+++ b/solution.py
@@ -338,10 +338,10 @@
 
 
 def settle_kernel(*refs):
-    ins, outs, sems = refs[:4], refs[4:8], refs[8]
+    ins, outs, sems, last = refs[:5], refs[5:10], refs[10], refs[11]
     pieces = sems.shape[1]
-    copies = []
-    for a, (src, dst) in enumerate(zip(ins, outs)):
+    copies = [pltpu.make_async_copy(ins[4], outs[4], last)]
+    for a, (src, dst) in enumerate(zip(ins[:4], outs[:4])):
         rows = src.shape[0] // pieces
         for i in range(pieces):
             part = pl.ds(i * rows, rows)
@@ -353,13 +353,13 @@
 
 
 def settle(*arrays):
-    anywhere = pl.BlockSpec(memory_space=pl.ANY)
     return pl.pallas_call(
         settle_kernel,
         out_shape=[jax.ShapeDtypeStruct(x.shape, x.dtype) for x in arrays],
-        in_specs=[anywhere] * 4,
-        out_specs=[pl.BlockSpec(memory_space=pltpu.HBM)] * 4,
-        scratch_shapes=[pltpu.SemaphoreType.DMA((4, 2))],
+        in_specs=[pl.BlockSpec(memory_space=pltpu.VMEM)] * 5,
+        out_specs=[pl.BlockSpec(memory_space=pltpu.HBM)] * 5,
+        scratch_shapes=[pltpu.SemaphoreType.DMA((4, 2)), pltpu.SemaphoreType.DMA],
+        compiler_params=pltpu.CompilerParams(vmem_limit_bytes=6 * 2**20),
         name="settle",
     )(*arrays)
 
@@ -422,7 +422,7 @@
             for x in (queries[0], keys[0], values[0], adjoint[0], listing[0].T, sharpness)
         )
     )
-    o, dq, dk, dv = settle(o, dq, dk, dv)
+    o, dq, dk, dv, ds = settle(o, dq, dk, dv, ds)
     return o[None], dq[None], dk[None], dv[None], ds[0]
 
 

time: 329 us -> 199 us (0.60)
  Pallas kernels: 324 us -> 198 us
  local copies, waits for them, and re-layouts: 4.46 us -> 0 us
    pallas_call x1, Pallas kernels: 128 us -> 2.09 us  [settle(): pl.pallas_call(settle_kernel, out_shape=[jax.ShapeDtypeStruct(x.shape, x....]
    unnamed x9 -> x0, local copies, waits for them, and re-layouts: 4.46 us -> none
where the time goes in v3:
time: 199 us
  Pallas kernels  198 us (99%)
    pallas_call x1, Pallas kernels, per_device(): pl.pallas_call(functools.partial(kernel, chips, dps), out_shape=[whole] *...  196 us

profile of v3, /device:TPU:1, one launch (start us, length us, event | category | flops | bytes accessed | tf_op | source)
XLA Modules:
  0.0 198.6 jit_solution(2314539157560722354)
XLA Ops:
  0.6 195.9 %attend.1 = (f32[128,2048]{1,0:T(8,128)S(1)}, f32[128,2048]{1,0:T(8,128)S(1)}, f32[128,2048]{1,0:T(8,128)S(1)}, f32[128,2048]{1,0:T(8,128)S(1)}, f32[1,16]{1,0:T(1,128)S(1)}) custom-call(f32[128,2048]{1,0:T(8,128)} %bitcast.12, f32[128,2048]{1,0:T(8,128)} %bitcast.13, f32[128,2048]{1,0:T(8,128)} %bitcast.14, f32[128,2048]{1,0:T(8,128)} %bitcast.15, ...), custom_call_target="tpu_custom_call" | custom-call | tf_op jit(solution)/shard_map/attend/pallas_call | solution.py:377
  196.5 2.1 %settle.1 = (f32[128,2048]{1,0:T(8,128)}, f32[128,2048]{1,0:T(8,128)}, f32[128,2048]{1,0:T(8,128)}, f32[128,2048]{1,0:T(8,128)}, f32[1,16]{1,0:T(1,128)}) custom-call(f32[128,2048]{1,0:T(8,128)S(1)} %get-tuple-element.15.refs_0_, f32[128,2048]{1,0:T(8,128)S(1)} %get-tuple-element.16.refs_1_, f32[128,2048]{1,0:T(8,128)S(1)} %get-tuple-element.17.refs_2_, ...), custom_call_target="tpu_custom_call" | custom-call | tf_op jit(solution)/shard_map/settle/pallas_call | solution.py:356

commit v4 on v3

--- a/solution.py
+++ b/solution.py
@@ -273,15 +273,25 @@
     for i in range(2):
         pltpu.make_async_copy(part.at[i], part.at[i], recv_part.at[i]).wait()
 
-    def finish(t, _):
-        j = slot_of(t)
+    def order(t):
+        i = t // 4
+        r = t % 4
+        return jnp.where(r == 0, (4 * i + 2), jnp.where(r == 1, 4 * i + 1, jnp.where(r == 2, (4 * i + 8) % 16, 4 * i + 3)))
+
+    def finish_k(t, _):
+        j = slot_of(order(t))
         dk[s, j] = gather(dk, runk, s, j) + part[0, j]
+        put(j, dk.at[s, j], columns(dk_ref, head), send_dkv, recv_out.at[2])
+        return _
+
+    def finish_v(t, _):
+        j = slot_of(order(t))
         dv[s, j] = gather(dv, runv, s, j) + part[1, j]
-        put(j, dk.at[s, j], columns(dk_ref, head), send_dkv, recv_out.at[2])
         put(j, dv.at[s, j], columns(dv_ref, head), send_dkv, recv_out.at[3])
         return _
 
-    lax.fori_loop(0, heads, finish, None)
+    lax.fori_loop(0, heads, finish_k, None)
+    lax.fori_loop(0, heads, finish_v, None)
 
     pltpu.make_async_copy(sh_all, sh_all, recv_small.at[3]).wait()
     dp_all[dp] = sh_all[:, 0, :]

time: 199 us -> 197 us (0.990)
  Pallas kernels: 198 us -> 196 us
where the time goes in v4:
time: 197 us
  Pallas kernels  196 us (99%)
    pallas_call x1, Pallas kernels, per_device(): pl.pallas_call(functools.partial(kernel, chips, dps), out_shape=[whole] *...  194 us

profile of v4, /device:TPU:1, one launch (start us, length us, event | category | flops | bytes accessed | tf_op | source)
XLA Modules:
  0.0 197.0 jit_solution(7525780972035411815)
XLA Ops:
  0.6 194.3 %attend.1 = (f32[128,2048]{1,0:T(8,128)S(1)}, f32[128,2048]{1,0:T(8,128)S(1)}, f32[128,2048]{1,0:T(8,128)S(1)}, f32[128,2048]{1,0:T(8,128)S(1)}, f32[1,16]{1,0:T(1,128)S(1)}) custom-call(f32[128,2048]{1,0:T(8,128)} %bitcast.12, f32[128,2048]{1,0:T(8,128)} %bitcast.13, f32[128,2048]{1,0:T(8,128)} %bitcast.14, f32[128,2048]{1,0:T(8,128)} %bitcast.15, ...), custom_call_target="tpu_custom_call" | custom-call | tf_op jit(solution)/shard_map/attend/pallas_call | solution.py:387
  194.9 2.1 %settle.1 = (f32[128,2048]{1,0:T(8,128)}, f32[128,2048]{1,0:T(8,128)}, f32[128,2048]{1,0:T(8,128)}, f32[128,2048]{1,0:T(8,128)}, f32[1,16]{1,0:T(1,128)}) custom-call(f32[128,2048]{1,0:T(8,128)S(1)} %get-tuple-element.15.refs_0_, f32[128,2048]{1,0:T(8,128)S(1)} %get-tuple-element.16.refs_1_, f32[128,2048]{1,0:T(8,128)S(1)} %get-tuple-element.17.refs_2_, ...), custom_call_target="tpu_custom_call" | custom-call | tf_op jit(solution)/shard_map/settle/pallas_call | solution.py:366

commit v5 on v4

--- a/solution.py
+++ b/solution.py
@@ -252,14 +252,14 @@
         at = lasts[2 * i + half]
         return total[half, i] + jnp.where(at >= 0, run[jnp.maximum(at, 0)], 0.0)
 
-    def far_sibling(i, _):
-        dk[1 - s, i] = gather(dk, runk, 1 - s, i)
-        dv[1 - s, i] = gather(dv, runv, 1 - s, i)
-        return _
-
-    lax.fori_loop(0, heads, far_sibling, None)
-    for i, ref in enumerate((dk, dv)):
-        to_sibling(ref.at[1 - s], part.at[i], send_part.at[i], recv_part.at[i]).start()
+    for a, (total, run) in enumerate(((dk, runk), (dv, runv))):
+
+        def far_sibling(i, _, total=total, run=run):
+            total[1 - s, i] = gather(total, run, 1 - s, i)
+            return _
+
+        lax.fori_loop(0, heads, far_sibling, None)
+        to_sibling(total.at[1 - s], part.at[a], send_part.at[a], recv_part.at[a]).start()
 
     small.wait()
     sh_tot[...] = sh_own[...] + sh_sib[...]
@@ -269,9 +269,6 @@
         return _
 
     lax.fori_loop(0, heads, send_sharp, None)
-
-    for i in range(2):
-        pltpu.make_async_copy(part.at[i], part.at[i], recv_part.at[i]).wait()
 
     def order(t):
         i = t // 4
@@ -290,8 +287,9 @@
         put(j, dv.at[s, j], columns(dv_ref, head), send_dkv, recv_out.at[3])
         return _
 
-    lax.fori_loop(0, heads, finish_k, None)
-    lax.fori_loop(0, heads, finish_v, None)
+    for i, finish in enumerate((finish_k, finish_v)):
+        pltpu.make_async_copy(part.at[i], part.at[i], recv_part.at[i]).wait()
+        lax.fori_loop(0, heads, finish, None)
 
     pltpu.make_async_copy(sh_all, sh_all, recv_small.at[3]).wait()
     dp_all[dp] = sh_all[:, 0, :]

time: 197 us -> 197 us (level)
  no operation moved by 1% of the time
where the time goes in v5:
time: 197 us
  Pallas kernels  197 us (100%)
    pallas_call x1, Pallas kernels, per_device(): pl.pallas_call(functools.partial(kernel, chips, dps), out_shape=[whole] *...  194 us

profile of v5, /device:TPU:1, one launch (start us, length us, event | category | flops | bytes accessed | tf_op | source)
XLA Modules:
  0.0 197.2 jit_solution(3231426498225513474)
XLA Ops:
  0.6 194.5 %attend.1 = (f32[128,2048]{1,0:T(8,128)S(1)}, f32[128,2048]{1,0:T(8,128)S(1)}, f32[128,2048]{1,0:T(8,128)S(1)}, f32[128,2048]{1,0:T(8,128)S(1)}, f32[1,16]{1,0:T(1,128)S(1)}) custom-call(f32[128,2048]{1,0:T(8,128)} %bitcast.12, f32[128,2048]{1,0:T(8,128)} %bitcast.13, f32[128,2048]{1,0:T(8,128)} %bitcast.14, f32[128,2048]{1,0:T(8,128)} %bitcast.15, ...), custom_call_target="tpu_custom_call" | custom-call | tf_op jit(solution)/shard_map/attend/pallas_call | solution.py:385
  195.1 2.1 %settle.1 = (f32[128,2048]{1,0:T(8,128)}, f32[128,2048]{1,0:T(8,128)}, f32[128,2048]{1,0:T(8,128)}, f32[128,2048]{1,0:T(8,128)}, f32[1,16]{1,0:T(1,128)}) custom-call(f32[128,2048]{1,0:T(8,128)S(1)} %get-tuple-element.15.refs_0_, f32[128,2048]{1,0:T(8,128)S(1)} %get-tuple-element.16.refs_1_, f32[128,2048]{1,0:T(8,128)S(1)} %get-tuple-element.17.refs_2_, ...), custom_call_target="tpu_custom_call" | custom-call | tf_op jit(solution)/shard_map/settle/pallas_call | solution.py:364
